TPU v7x, 32 devices: a whole 2x2x4 slice. The times are simulated.
32 devices in a mesh: mp: 4 (over z), store: 4 (over x, core), group: 2 (over y).
Axes of the slice: x: 2, y: 2, z: 4, core: 2. Of those that a mesh axis runs over, the one named last changes fastest.
Arguments:
- gate_pre: bfloat16 [8, 1024, 14336], P(('store', 'group'), None, 'mp'), may hold values from -6 to 6
- up_pre: bfloat16 [8, 1024, 14336], P(('store', 'group'), None, 'mp'), may hold values from -6 to 6
- out_grad: bfloat16 [8, 1024, 8192], P(('store', 'group'), 'mp'), may hold values from -6 to 6
- normed_in: bfloat16 [8, 1024, 8192], P(('store', 'group'), 'mp'), may hold values from -6 to 6
- lengths: int32 [8, 16], P(('store', 'group')), may hold values from 1 to 128, 1024 in all within a row
- w_down: bfloat16 [14336, 8192], P('mp'), may hold values from -0.046875 to 0.046875
- proj_hidden: bfloat16 [14336, 64], P('mp'), may hold values from -0.046875 to 0.046875
- proj_gate: bfloat16 [14336, 64], P('mp'), may hold values from -0.046875 to 0.046875
- proj_up: bfloat16 [14336, 64], P('mp'), may hold values from -0.046875 to 0.046875
- proj_outgrad: bfloat16 [8192, 64], replicated, may hold values from -0.0625 to 0.0625
- proj_input: bfloat16 [8192, 64], replicated, may hold values from -0.0625 to 0.0625
- datastore: bfloat16 [16384, 12288], P(('store', 'group'), 'mp'), may hold values from -0.011962891 to 0.011962891
Outputs:
- scores: float32 [128, 16384], P('mp', ('store', 'group'))
Inputs may be any that keep to these rules, and one draw needn't show every extreme that they name: Each row holds 16 lengths of 1 or more summing to 1024; the longest of each row is exactly 128.
All inputs are finite; a program needn't handle non-finite values.
Results may differ from a plain program's by a relative error of at most 0.0041.
Values may be sent and summed in bfloat16 or wider, within the bound.
A program may use at most 192 MiB of HBM per device.

v0:
```python
import jax
import jax.numpy as jnp
from jax import lax
from jax.sharding import PartitionSpec as P


def membership(seq_starts, seq_ends, count):
    positions = jnp.arange(count, dtype=jnp.int32)
    return (
        (positions[:, None] >= seq_starts[None, :]) & (positions[:, None] < seq_ends[None, :])
    ).astype(jnp.float32)


def outer_sums(member, left, right):
    weighted = (member[:, :, None] * left[:, None, :]).reshape(left.shape[0], -1)
    summed = lax.dot_general(
        weighted,
        right,
        (((0,), (0,)), ((), ())),
        precision=lax.Precision.HIGHEST,
        preferred_element_type=jnp.float32,
    )
    return summed.reshape(member.shape[1], -1)


def on_device(
    gate_pre,
    up_pre,
    out_grad,
    normed_in,
    lengths,
    w_down,
    proj_hidden,
    proj_gate,
    proj_up,
    proj_outgrad,
    proj_input,
    datastore,
):
    gate_val = gate_pre[0].astype(jnp.float32)
    up_val = up_pre[0].astype(jnp.float32)
    gate_sig = jax.nn.sigmoid(gate_val)
    silu_gate = gate_val * gate_sig
    hidden = (silu_gate * up_val).astype(jnp.bfloat16)
    grad_own = out_grad[0]
    input_own = normed_in[0]
    hidden_grad = lax.dot_general(
        lax.all_gather(grad_own, "mp", axis=0, tiled=True),
        w_down,
        (((1,), (1,)), ((), ())),
        preferred_element_type=jnp.float32,
    )
    gate_grad = (hidden_grad * up_val * gate_sig * (1.0 + gate_val * (1.0 - gate_sig))).astype(
        jnp.bfloat16
    )
    up_grad = (hidden_grad * silu_gate).astype(jnp.bfloat16)
    down_in_part = jnp.dot(hidden, proj_hidden, preferred_element_type=jnp.float32)
    gate_out_part = jnp.dot(gate_grad, proj_gate, preferred_element_type=jnp.float32)
    up_out_part = jnp.dot(up_grad, proj_up, preferred_element_type=jnp.float32)
    down_out_own = jnp.dot(grad_own, proj_outgrad, preferred_element_type=jnp.float32)
    gate_in_own = jnp.dot(input_own, proj_input, preferred_element_type=jnp.float32)
    example_lengths = lengths[0]
    order = jnp.arange(example_lengths.shape[0], dtype=jnp.int32)
    seq_ends = jnp.sum(
        jnp.where(order[None, :] <= order[:, None], example_lengths[None, :], 0), axis=1
    )
    seq_starts = seq_ends - example_lengths
    all_count = gate_val.shape[0]
    gate_in, down_out = (
        lax.all_gather(gate_in_own, "mp", axis=0, tiled=True),
        lax.all_gather(down_out_own, "mp", axis=0, tiled=True),
    )
    member = membership(seq_starts, seq_ends, all_count)
    partial_value = jnp.concatenate(
        [
            outer_sums(member, down_in_part, down_out),
            outer_sums(member, gate_in, gate_out_part),
            outer_sums(member, gate_in, up_out_part),
        ],
        axis=1,
    )
    feats = lax.psum_scatter(partial_value, "mp", scatter_dimension=1, tiled=True).astype(
        jnp.bfloat16
    )
    queries = lax.all_gather(feats, ("store", "group"), axis=0, tiled=True)
    partial_scores = lax.dot_general(
        queries, datastore, (((1,), (1,)), ((), ())), preferred_element_type=jnp.float32
    )
    return lax.psum_scatter(partial_scores, "mp", scatter_dimension=0, tiled=True)


def solution(mesh):
    return jax.shard_map(
        on_device,
        mesh=mesh,
        in_specs=(
            P(("store", "group"), None, "mp"),
            P(("store", "group"), None, "mp"),
            P(("store", "group"), "mp", None),
            P(("store", "group"), "mp", None),
            P(("store", "group"), None),
            P("mp", None),
            P("mp", None),
            P("mp", None),
            P("mp", None),
            P(),
            P(),
            P(("store", "group"), "mp"),
        ),
        out_specs=P("mp", ("store", "group")),
        check_vma=False,
    )
```

profile of v0, /device:TPU:0, one launch (start us, length us, event | category | flops | bytes accessed | tf_op | source)
XLA Modules:
  0.0 488.7 jit_solution(17629856953622826828)
XLA Ops:
  6.5 0.0 copy-start
  6.5 0.0 copy-start.7
  6.5 0.0 copy-start.4
  6.5 0.0 all-gather.3.cloned.1.call-start
  6.5 0.7 all-gather.3.cloned.1.call-update
  7.3 0.0 reduce-scatter.3.cloned.1.call-start
  7.3 0.5 copy-done
  7.8 3.6 fusion.18
  11.3 16.2 %all_gather.12 = f32[1024,64]{0,1:T(8,128)S(1)} all-gather(f32[256,64]{0,1:T(8,128)S(1)} %fusion.18), channel_id=1, replica_groups=mesh['mp'=4,'store'=4,'group'=2] {'mp'}, dimensions={0}, use_global_device_ids=true | all-gather | bytes 327680 | tf_op jit(solution)/shard_map/all_gather | solution.py:71
  27.5 4.4 fusion.16
  31.9 25.6 %all_gather.13 = f32[1024,64]{0,1:T(8,128)S(1)} all-gather(f32[256,64]{0,1:T(8,128)S(1)} %fusion.16), channel_id=1, replica_groups=mesh['mp'=4,'store'=4,'group'=2] {'mp'}, dimensions={0}, use_global_device_ids=true | all-gather | bytes 327680 | tf_op jit(solution)/shard_map/all_gather | solution.py:70
  57.5 0.0 copy-done.7
  57.5 0.1 select_reduce_fusion
  57.6 0.1 fusion.21
  57.7 0.0 copy-done.4
  57.7 7.9 %fusion.11 = f32[1024,64]{0,1:T(8,128)S(1)} fusion(bf16[3584,64]{0,1:T(8,128)(2,1)S(1)} %copy-done.4, bf16[1,1024,3584]{2,1,0:T(8,128)(2,1)} %param.13, bf16[1,1024,3584]{2,1,0:T(8,128)(2,1)} %param.12), kind=kOutput, calls=%fused_computation.17 | convolution fusion | flops 499122176 | bytes 15400960 | tf_op jit(solution)/shard_map/dot_general | solution.py:57
  65.6 3.1 broadcast_multiply_fusion.1
  68.7 3.4 fusion.26
  72.1 0.9 reshape.65
  72.9 0.0 copy-start.5
  73.0 229.7 %all-gather.3.cloned.1.call-done = bf16[1,1024,8192]{2,1,0:T(8,128)(2,1)} async-done(((bf16[1,256,8192]{2,1,0:T(8,128)(2,1)}), bf16[1,1024,8192]{2,1,0:T(8,128)(2,1)}) %all-gather.3.cloned.1.call-update) | async-done | bytes 16777232 | tf_op jit(solution)/shard_map/all_gather | solution.py:48
  302.6 71.4 %fusion = f32[1024,3584]{1,0:T(8,128)} fusion(bf16[3584,8192]{1,0:T(8,128)(2,1)} %param.17, bf16[1,1024,8192]{2,1,0:T(8,128)(2,1)} %all-gather.3.cloned.1.call-done), kind=kOutput, calls=%fused_computation.5 | convolution fusion | flops 60129542144 | bytes 90177536 | tf_op jit(solution)/shard_map/dot_general | solution.py:47
  374.1 0.0 copy-done.5
  374.1 0.0 copy-start.6
  374.1 9.4 %fusion.10 = f32[1024,64]{0,1:T(8,128)S(1)} fusion(bf16[3584,64]{0,1:T(8,128)(2,1)S(1)} %copy-done.5, f32[1024,3584]{1,0:T(8,128)} %fusion, bf16[1,1024,3584]{2,1,0:T(8,128)(2,1)} %param.12), kind=kOutput, calls=%fused_computation.16 | convolution fusion | flops 495452160 | bytes 22740992 | tf_op jit(solution)/shard_map/dot_general | solution.py:59
  383.5 0.0 copy-done.6
  383.5 0.0 copy-start.2
  383.5 0.0 copy-start.3
  383.5 12.9 %fusion.14 = f32[1024,64]{0,1:T(8,128)S(1)} fusion(bf16[3584,64]{0,1:T(8,128)(2,1)S(1)} %copy-done.6, f32[1024,3584]{1,0:T(8,128)} %fusion, bf16[1,1024,3584]{2,1,0:T(8,128)(2,1)} %param.13, bf16[1,1024,3584]{2,1,0:T(8,128)(2,1)} %param.12), kind=kOutput, calls=%fused_computation.19 | convolution fusion | flops 513802240 | bytes 30081024 | tf_op jit(solution)/shard_map/dot_general | solution.py:58
  396.5 0.0 copy-done.2
  396.5 0.0 copy-start.1
  396.5 3.4 fusion.28
  399.9 3.4 fusion.27
  403.3 0.2 reshape.66
  403.5 0.2 reshape.67
  403.7 0.0 copy-done.3
  403.7 0.9 pad_maximum_fusion
  404.6 0.0 reduce-scatter.3.cloned.1.call-update
  404.6 0.0 reduce-scatter.5.cloned.1.call-start
  404.7 22.1 %reduce-scatter.3.cloned.1.call-done = f32[16,3072]{1,0:T(8,128)} async-done(((f32[16,12288]{1,0:T(8,128)}), f32[16,3072]{1,0:T(8,128)}) %reduce-scatter.3.cloned.1.call-update) | async-done | bytes 196624 | tf_op jit(solution)/shard_map/reduce_scatter | solution.py:82
  426.8 0.9 convert_element_type.39
  427.7 18.4 %all_gather.15 = bf16[128,3072]{1,0:T(8,128)(2,1)S(1)} all-gather(bf16[16,3072]{1,0:T(8,128)(2,1)S(1)} %convert_element_type.39), channel_id=1, replica_groups=mesh['mp'=4,'store'=4,'group'=2] {'store','group'}, dimensions={0}, use_global_device_ids=true | all-gather | bytes 884736 | tf_op jit(solution)/shard_map/all_gather | solution.py:85
  446.2 9.8 %fusion.29 = f32[128,2048]{1,0:T(8,128)} fusion(bf16[128,3072]{1,0:T(8,128)(2,1)S(1)} %all_gather.15, bf16[2048,3072]{1,0:T(8,128)(2,1)} %param.23), kind=kOutput, calls=%fused_computation.41 | convolution fusion | flops 1610612736 | bytes 14417920 | tf_op jit(solution)/shard_map/dot_general | solution.py:86
  456.0 0.0 reduce-scatter.5.cloned.1.call-update
  456.0 26.1 %reduce-scatter.5.cloned.1.call-done = f32[32,2048]{1,0:T(8,128)} async-done(((f32[128,2048]{1,0:T(8,128)}), f32[32,2048]{1,0:T(8,128)}) %reduce-scatter.5.cloned.1.call-update) | async-done | bytes 262160 | tf_op jit(solution)/shard_map/reduce_scatter | solution.py:89
  482.2 0.0 copy-done.1
  (1 shorter events, 0.0 us)
Async XLA Ops:
  6.5 1.2 copy-start
  6.5 50.9 %copy-start.7 = (s32[1,16]{1,0:T(1,128)S(1)}, s32[1,16]{1,0:T(1,128)}, u32[]{:S(2)}) copy-start(s32[1,16]{1,0:T(1,128)} %param.16) | copy-start | bytes 196
  6.5 51.1 %copy-start.4 = (bf16[3584,64]{0,1:T(8,128)(2,1)S(1)}, bf16[3584,64]{0,1:T(8,128)(2,1)}, u32[]{:S(2)}) copy-start(bf16[3584,64]{0,1:T(8,128)(2,1)} %param.18) | copy-start | bytes 1376260
  6.5 296.1 %all-gather.3.cloned.1.call-start = ((), (), s32[]{:S(2)}) async-start(), calls=%async_computation.4 | async-start | bytes 20971520 | tf_op jit(solution)/shard_map/all_gather | solution.py:48
  7.3 419.5 %reduce-scatter.3.cloned.1.call-start = ((), (), s32[]{:S(2)}) async-start(), calls=%async_computation.2 | async-start | bytes 983040 | tf_op jit(solution)/shard_map/reduce_scatter | solution.py:82
  72.9 301.1 %copy-start.5 = (bf16[3584,64]{0,1:T(8,128)(2,1)S(1)}, bf16[3584,64]{0,1:T(8,128)(2,1)}, u32[]{:S(2)}) copy-start(bf16[3584,64]{0,1:T(8,128)(2,1)} %param.20) | copy-start | bytes 1376260
  374.1 9.5 %copy-start.6 = (bf16[3584,64]{0,1:T(8,128)(2,1)S(1)}, bf16[3584,64]{0,1:T(8,128)(2,1)}, u32[]{:S(2)}) copy-start(bf16[3584,64]{0,1:T(8,128)(2,1)} %param.19) | copy-start | bytes 1376260
  383.5 13.0 %copy-start.2 = (f32[1024,16,64]{0,2,1:T(8,128)S(1)}, f32[1024,16,64]{0,2,1:T(8,128)}, u32[]{:S(2)}) copy-start(f32[1024,16,64]{0,2,1:T(8,128)} %get-tuple-element.6) | copy-start | bytes 12582916
  383.5 20.1 %copy-start.3 = (f32[16,4096]{1,0:T(8,128)S(1)}, f32[16,4096]{1,0:T(8,128)}, u32[]{:S(2)}) copy-start(f32[16,4096]{1,0:T(8,128)} %reshape.65) | copy-start | bytes 786436
  396.5 85.7 %copy-start.1 = (bf16[8192,64]{0,1:T(8,128)(2,1)S(1)}, bf16[8192,64]{0,1:T(8,128)(2,1)}, u32[]{:S(2)}) copy-start(bf16[8192,64]{0,1:T(8,128)(2,1)} %param.21) | copy-start | bytes 3145732
  404.6 77.5 %reduce-scatter.5.cloned.1.call-start = ((), (), s32[]{:S(2)}) async-start(), calls=%async_computation.3 | async-start | bytes 1310720 | tf_op jit(solution)/shard_map/reduce_scatter | solution.py:89
Sparse Core Ops, SparseCore 0:
  8.9 293.6 all-gather.2
  404.8 21.9 reduce-scatter.2
  456.2 25.9 reduce-scatter.4
where the time goes:
time: 489 us
  waiting for transfers between devices  279 us (57%)
  matrix products  130 us (27%)
  blocking collectives  60.2 us (12%)
  between operations  13.2 us (3%)
  other arithmetic  5.16 us (1%)
    all_gather x1, waiting for transfers between devices, on_device(): lax.all_gather(grad_own, 'mp', axis=0, tiled=True)  230 us
    dot_general x1, matrix products, on_device(): lax.dot_general(lax.all_gather(grad_own, 'mp', axis=0, tiled=True), w_dow...  71.4 us
    reduce_scatter x1, waiting for transfers between devices, on_device(): lax.psum_scatter(partial_scores, 'mp', scatter_dimension=0, tiled=True)  26.1 us
    all_gather x1, blocking collectives, on_device(): lax.all_gather(gate_in_own, 'mp', axis=0, tiled=True)  25.6 us
    reduce_scatter x1, waiting for transfers between devices, on_device(): lax.psum_scatter(partial_value, 'mp', scatter_dimension=1, tiled=True)  22.1 us
    all_gather x1, blocking collectives, on_device(): queries = lax.all_gather(feats, ('store', 'group'), axis=0, tiled=True)  18.4 us
    all_gather x1, blocking collectives, on_device(): lax.all_gather(down_out_own, 'mp', axis=0, tiled=True)  16.2 us
    dot_general x1, matrix products, on_device(): jnp.dot(gate_grad, proj_gate, preferred_element_type=jnp.float32)  12.9 us
  transfers between devices with their start and end apart: 3, of which 3 were waited for; matrix products, arithmetic and copies ran while one was open for 5% of the time, Pallas kernels for 0%

commit v1 on v0

v1 whole, which is shorter than its diff:
```python
import functools

import jax
import jax.numpy as jnp
from jax import lax
from jax.experimental import pallas as pl
from jax.experimental.pallas import tpu as pltpu
from jax.sharding import PartitionSpec as P

MESH = pl.DeviceIdType.MESH
NT = (((1,), (1,)), ((), ()))
VMEM_LIMIT = 56 * 2**20


def tile_of(size, most):
    return max(t for t in range(128, most + 1, 128) if size % t == 0)


def gather_kernel(
    n, chunks, tile,
    og, w, gate, up, ph, pg, pu, po, ni, pi,
    down_in, gate_out, up_out, down_out, gate_in,
    held, acc, gin, send_sem, recv_sem, local_sem, gin_send, gin_recv,
):
    d = lax.axis_index("mp")
    tokens, width = og.shape
    depth = width // chunks
    tiles = w.shape[0] // tile
    left, right = lax.rem(d + n - 1, n), lax.rem(d + 1, n)

    barrier = pltpu.get_barrier_semaphore()
    for k in range(1, n):
        pl.semaphore_signal(
            barrier, inc=1, device_id={"mp": lax.rem(d + k, n)}, device_id_type=MESH
        )
    pl.semaphore_wait(barrier, n - 1)

    def columns(c):
        return pl.ds(pl.multiple_of(c * depth, depth), depth)

    def rows(p):
        return pl.ds(pl.multiple_of(p * tokens, tokens), tokens)

    def local(c):
        return pltpu.make_async_copy(og.at[:, columns(c)], held.at[d, c], local_sem.at[c])

    def remote(way, p, c, own):
        return pltpu.make_async_remote_copy(
            src_ref=og.at[:, columns(c)] if own else held.at[p, c],
            dst_ref=held.at[p, c],
            send_sem=send_sem.at[way, p, c],
            recv_sem=recv_sem.at[p, c],
            device_id={"mp": left if way == 0 else right},
            device_id_type=MESH,
        )

    has_left, has_right = d > 0, d < n - 1

    def send_own(c, carry):
        @pl.when(has_left)
        def _():
            remote(0, d, c, True).start()

        @pl.when(has_right)
        def _():
            remote(1, d, c, True).start()

        local(c).start()
        return carry

    lax.fori_loop(0, chunks, send_own, 0)

    for ref in (down_in, gate_out, up_out, down_out):
        ref[...] = jnp.zeros_like(ref)

    def own_gate_in(ni_ref, pi_ref):
        part = jnp.dot(ni_ref[...], pi_ref[...], preferred_element_type=jnp.float32)
        first = pl.program_id(0) == 0

        @pl.when(first)
        def _():
            gin[d] = part

        @pl.when(jnp.logical_not(first))
        def _():
            gin[d] += part

    pltpu.emit_pipeline(
        own_gate_in,
        grid=(chunks,),
        in_specs=[
            pl.BlockSpec((tokens, depth), lambda c: (0, c)),
            pl.BlockSpec((depth, pi.shape[1]), lambda c: (c, 0)),
        ],
    )(ni, pi)

    def gin_copy(k):
        return pltpu.make_async_remote_copy(
            src_ref=gin.at[d],
            dst_ref=gin.at[d],
            send_sem=gin_send.at[k],
            recv_sem=gin_recv.at[k],
            device_id={"mp": lax.rem(d + k, n)},
            device_id_type=MESH,
        )

    for k in range(1, n):
        gin_copy(k).start()

    def wait_local(c, carry):
        local(c).wait()
        return carry

    lax.fori_loop(0, chunks, wait_local, 0)

    def step(s, carry):
        shards = (d + s, d - s)
        valid = (shards[0] < n, (s > 0) & (shards[1] >= 0))
        at = (jnp.minimum(shards[0], n - 1), jnp.maximum(shards[1], 0))
        onward = (has_left, has_right)

        def arrive(c):
            for way in range(2):
                @pl.when(valid[way] & (s > 0))
                def _():
                    remote(way, at[way], c, False).wait_recv()

                    @pl.when(onward[way])
                    def _():
                        remote(way, at[way], c, False).start()

            for way in range(2):
                @pl.when(valid[way])
                def _():
                    down_out[rows(at[way]), :] += jnp.dot(
                        held[at[way], c],
                        po[columns(c), :],
                        preferred_element_type=jnp.float32,
                    )

        def chunk(c, inner):
            arrive(c)

            def body(w_ref):
                j = pl.program_id(0)
                for way in range(2):
                    @pl.when(valid[way])
                    def _():
                        part = lax.dot_general(
                            held[at[way], c], w_ref[...], NT,
                            preferred_element_type=jnp.float32,
                        )

                        @pl.when(c == 0)
                        def _():
                            acc[way, j] = part

                        @pl.when(c > 0)
                        def _():
                            acc[way, j] += part

            pltpu.emit_pipeline(
                body,
                grid=(tiles,),
                in_specs=[pl.BlockSpec((tile, depth), lambda j: (j, c))],
            )(w)
            return inner

        lax.fori_loop(0, chunks - 1, chunk, 0)
        last = chunks - 1
        arrive(last)

        def finish(w_ref, g0, u0, g1, u1, ph_ref, pg_ref, pu_ref):
            j = pl.program_id(0)
            for way, g_ref, u_ref in ((0, g0, u0), (1, g1, u1)):
                @pl.when(valid[way])
                def _():
                    grad = acc[way, j] + lax.dot_general(
                        held[at[way], last], w_ref[...], NT,
                        preferred_element_type=jnp.float32,
                    )
                    g = g_ref[...].astype(jnp.float32)
                    u = u_ref[...].astype(jnp.float32)
                    sig = jax.nn.sigmoid(g)
                    silu = g * sig
                    hidden = (silu * u).astype(jnp.bfloat16)
                    gate_grad = (grad * u * sig * (1.0 + g * (1.0 - sig))).astype(jnp.bfloat16)
                    up_grad = (grad * silu).astype(jnp.bfloat16)
                    at_rows = rows(at[way])
                    for out, value, proj in (
                        (down_in, hidden, ph_ref),
                        (gate_out, gate_grad, pg_ref),
                        (up_out, up_grad, pu_ref),
                    ):
                        out[at_rows, :] += jnp.dot(
                            value, proj[...], preferred_element_type=jnp.float32
                        )

        elem = lambda way: pl.BlockSpec((tokens, tile), lambda j: (at[way], j))
        proj = pl.BlockSpec((tile, ph.shape[1]), lambda j: (j, 0))
        pltpu.emit_pipeline(
            finish,
            grid=(tiles,),
            in_specs=[
                pl.BlockSpec((tile, depth), lambda j: (j, last)),
                elem(0), elem(0), elem(1), elem(1), proj, proj, proj,
            ],
        )(w, gate, up, gate, up, ph, pg, pu)
        return carry

    lax.fori_loop(0, n, step, 0)

    for k in range(1, n):
        gin_copy(k).wait()
    for p in range(n):
        gate_in[p * tokens:(p + 1) * tokens, :] = gin[p]

    def drain(p, carry):
        def one(c, inner):
            @pl.when(has_left & (p >= d))
            def _():
                remote(0, p, c, False).wait_send()

            @pl.when(has_right & (p <= d))
            def _():
                remote(1, p, c, False).wait_send()

            return inner

        return lax.fori_loop(0, chunks, one, carry)

    lax.fori_loop(0, n, drain, 0)


def gathered(n, og, w, gate, up, ph, pg, pu, po, ni, pi):
    tokens, width = og.shape
    units, r = ph.shape
    chunks = 4
    depth = width // chunks
    tile = tile_of(units, 512)
    out = jax.ShapeDtypeStruct((n * tokens, r), jnp.float32)
    hbm = pl.BlockSpec(memory_space=pl.ANY)
    vmem = pl.BlockSpec(memory_space=pltpu.VMEM)
    return pl.pallas_call(
        functools.partial(gather_kernel, n, chunks, tile),
        out_shape=[out] * 5,
        in_specs=[hbm] * 7 + [vmem, hbm, hbm],
        out_specs=[vmem] * 5,
        scratch_shapes=[
            pltpu.VMEM((n, chunks, tokens, depth), jnp.bfloat16),
            pltpu.VMEM((2, units // tile, tokens, tile), jnp.float32),
            pltpu.VMEM((n, tokens, r), jnp.float32),
            pltpu.SemaphoreType.DMA((2, n, chunks)),
            pltpu.SemaphoreType.DMA((n, chunks)),
            pltpu.SemaphoreType.DMA((chunks,)),
            pltpu.SemaphoreType.DMA((n,)),
            pltpu.SemaphoreType.DMA((n,)),
        ],
        compiler_params=pltpu.CompilerParams(
            collective_id=0, has_side_effects=True, vmem_limit_bytes=VMEM_LIMIT
        ),
        name="gather_grads",
    )(og, w, gate, up, ph, pg, pu, po, ni, pi)


def score_kernel(
    n, stores, groups, tile,
    parts, store_rows, out,
    feats_in, queries, store_buf, sent, own, back_in,
    store_sem, fs, fr, qs, qr, bs, br,
):
    d = lax.axis_index("mp")
    sx, gx = lax.axis_index("store"), lax.axis_index("group")
    me = sx * groups + gx
    replicas = stores * groups
    examples = parts.shape[1]
    block = own.shape[0]

    load = pltpu.make_async_copy(store_rows, store_buf, store_sem)
    load.start()

    def peer(k):
        return {"mp": lax.rem(d + k, n)}

    def mate(k):
        other = lax.rem(me + k, replicas)
        return {"store": other // groups, "group": lax.rem(other, groups)}

    barrier = pltpu.get_barrier_semaphore()
    for k in range(1, n):
        pl.semaphore_signal(barrier, inc=1, device_id=peer(k), device_id_type=MESH)
    for k in range(1, replicas):
        pl.semaphore_signal(barrier, inc=1, device_id=mate(k), device_id_type=MESH)
    pl.semaphore_wait(barrier, n + replicas - 2)

    def feats_copy(k):
        return pltpu.make_async_remote_copy(
            src_ref=parts.at[lax.rem(d + k, n)], dst_ref=feats_in.at[k - 1],
            send_sem=fs.at[k - 1], recv_sem=fr.at[k - 1],
            device_id=peer(k), device_id_type=MESH,
        )

    for k in range(1, n):
        feats_copy(k).start()
    total = parts[d].astype(jnp.float32)
    for k in range(1, n):
        feats_copy(k).wait_recv()
        total += feats_in[k - 1].astype(jnp.float32)
    my_rows = pl.ds(pl.multiple_of(me * examples, examples), examples)
    queries[my_rows, :] = total.astype(jnp.bfloat16)

    def query_copy(k):
        return pltpu.make_async_remote_copy(
            src_ref=queries.at[my_rows, :], dst_ref=queries.at[my_rows, :],
            send_sem=qs.at[k - 1], recv_sem=qr.at[k - 1],
            device_id=mate(k), device_id_type=MESH,
        )

    for k in range(1, replicas):
        query_copy(k).start()
    load.wait()
    for k in range(1, replicas):
        query_copy(k).wait_recv()

    def scores(j, carry):
        cols = pl.ds(pl.multiple_of(j * tile, tile), tile)
        part = lax.dot_general(
            queries[...], store_buf[cols, :], NT, preferred_element_type=jnp.float32
        )
        for p in range(n):
            piece = part[p * block:(p + 1) * block, :]
            sent[p, :, cols] = piece.astype(sent.dtype)

            @pl.when(p == d)
            def _():
                own[:, cols] = piece

        return carry

    lax.fori_loop(0, store_buf.shape[0] // tile, scores, 0)

    def back_copy(k):
        return pltpu.make_async_remote_copy(
            src_ref=sent.at[lax.rem(d + k, n)], dst_ref=back_in.at[k - 1],
            send_sem=bs.at[k - 1], recv_sem=br.at[k - 1],
            device_id=peer(k), device_id_type=MESH,
        )

    for k in range(1, n):
        back_copy(k).start()
    for k in range(1, n):
        back_copy(k).wait_recv()
        own[...] += back_in[k - 1].astype(jnp.float32)
    out[...] = own[...]
    for k in range(1, n):
        feats_copy(k).wait_send()
        back_copy(k).wait_send()
    for k in range(1, replicas):
        query_copy(k).wait_send()


def scored(n, stores, groups, parts, datastore):
    _, examples, width = parts.shape
    count = datastore.shape[0]
    replicas = stores * groups
    block = replicas * examples // n
    sent = jnp.bfloat16 if block % 16 == 0 else jnp.float32
    vmem = pl.BlockSpec(memory_space=pltpu.VMEM)
    dma = pltpu.SemaphoreType.DMA
    return pl.pallas_call(
        functools.partial(score_kernel, n, stores, groups, tile_of(count, 512)),
        out_shape=jax.ShapeDtypeStruct((block, count), jnp.float32),
        in_specs=[vmem, pl.BlockSpec(memory_space=pl.ANY)],
        out_specs=vmem,
        scratch_shapes=[
            pltpu.VMEM((n - 1, examples, width), jnp.bfloat16),
            pltpu.VMEM((replicas * examples, width), jnp.bfloat16),
            pltpu.VMEM(datastore.shape, jnp.bfloat16),
            pltpu.VMEM((n, block, count), sent),
            pltpu.VMEM((block, count), jnp.float32),
            pltpu.VMEM((n - 1, block, count), sent),
            dma(()), dma((n - 1,)), dma((n - 1,)),
            dma((replicas - 1,)), dma((replicas - 1,)),
            dma((n - 1,)), dma((n - 1,)),
        ],
        compiler_params=pltpu.CompilerParams(
            collective_id=1, has_side_effects=True, vmem_limit_bytes=VMEM_LIMIT
        ),
        name="exchange_scores",
    )(parts, datastore)


def outer_sums(member, left, right):
    weighted = (member[:, :, None] * left[:, None, :]).reshape(left.shape[0], -1)
    summed = lax.dot_general(
        weighted,
        right,
        (((0,), (0,)), ((), ())),
        precision=lax.Precision.HIGHEST,
        preferred_element_type=jnp.float32,
    )
    return summed.reshape(member.shape[1], left.shape[1], right.shape[1])


def on_device(
    n, stores, groups,
    gate_pre, up_pre, out_grad, normed_in, lengths, w_down,
    proj_hidden, proj_gate, proj_up, proj_outgrad, proj_input, datastore,
):
    count = gate_pre.shape[1]
    r = proj_hidden.shape[1]
    example_lengths = lengths[0]
    examples = example_lengths.shape[0]
    order = jnp.arange(examples, dtype=jnp.int32)
    ends = jnp.sum(
        jnp.where(order[None, :] <= order[:, None], example_lengths[None, :], 0), axis=1
    )
    starts = ends - example_lengths
    positions = jnp.arange(count, dtype=jnp.int32)
    member = (
        (positions[:, None] >= starts[None, :]) & (positions[:, None] < ends[None, :])
    ).astype(jnp.float32)

    down_in, gate_out, up_out, down_out, gate_in = gathered(
        n, out_grad[0], w_down, gate_pre[0], up_pre[0],
        proj_hidden, proj_gate, proj_up, proj_outgrad, normed_in[0], proj_input,
    )
    down = outer_sums(member, down_in, down_out)
    both = outer_sums(member, gate_in, jnp.concatenate([gate_out, up_out], axis=1))
    feats = jnp.concatenate([down, both[:, :, :r], both[:, :, r:]], axis=1)
    parts = (
        feats.astype(jnp.bfloat16)
        .reshape(examples, n, -1)
        .transpose(1, 0, 2)
    )
    return scored(n, stores, groups, parts, datastore)


def solution(mesh):
    sizes = mesh.shape
    return jax.shard_map(
        functools.partial(on_device, sizes["mp"], sizes["store"], sizes["group"]),
        mesh=mesh,
        in_specs=(
            P(("store", "group"), None, "mp"),
            P(("store", "group"), None, "mp"),
            P(("store", "group"), "mp", None),
            P(("store", "group"), "mp", None),
            P(("store", "group"), None),
            P("mp", None),
            P("mp", None),
            P("mp", None),
            P("mp", None),
            P(),
            P(),
            P(("store", "group"), "mp"),
        ),
        out_specs=P("mp", ("store", "group")),
        check_vma=False,
    )
```

time: 489 us -> 369 us (0.75)
  Pallas kernels: 0 us -> 338 us
  waiting for transfers between devices: 279 us -> 0 us
  matrix products: 130 us -> 13.9 us
  blocking collectives: 60.2 us -> 0 us
  between operations: 13.2 us -> 0.12 us
  local copies, waits for them, and re-layouts: 1.74 us -> 14.3 us
    pallas_call x0 -> x2, Pallas kernels: none -> 338 us  [the longest x1 301 us: gathered(): pl.pallas_call(functools.partial(gather_kernel, n, chunks, tile), out_sha...]
    all_gather x1 -> x0, waiting for transfers between devices: 230 us -> none  [on_device(): lax.all_gather(grad_own, 'mp', axis=0, tiled=True)]
    dot_general x7 -> x0, matrix products: 119 us -> none  [the longest x1 71.4 us: on_device(): lax.dot_general(lax.all_gather(grad_own, 'mp', axis=0, tiled=True), w_dow...]
    all_gather x3 -> x0, blocking collectives: 60.2 us -> none  [the longest x1 25.6 us: on_device(): lax.all_gather(gate_in_own, 'mp', axis=0, tiled=True)]
    reduce_scatter x2 -> x0, waiting for transfers between devices: 48.3 us -> none  [the longest x1 26.1 us: on_device(): lax.psum_scatter(partial_scores, 'mp', scatter_dimension=0, tiled=True)]
    unnamed x16 -> x18, local copies, waits for them, and re-layouts: 0.48 us -> 11 us
    dot_general x3 -> x2, matrix products: 10.2 us -> 13.9 us  [outer_sums(): lax.dot_general(weighted, right, (((0,), (0,)), ((), ())), precision=lax....]
  transfers between devices with their start and end apart: 3 -> 0, of which waited for: 3 -> 0; matrix products, arithmetic and copies ran while one was open for 5% -> 0% of each run, Pallas kernels for 0% -> 0%
where the time goes in v1:
time: 369 us; the launch traced here: 367 us
  Pallas kernels  338 us (92%)
  local copies, waits for them, and re-layouts  14.3 us (4%)
  matrix products  13.9 us (4%)
    pallas_call x1, Pallas kernels, gathered(): pl.pallas_call(functools.partial(gather_kernel, n, chunks, tile), out_sha...  301 us
    pallas_call x1, Pallas kernels, scored(): pl.pallas_call(functools.partial(score_kernel, n, stores, groups, tile_of...  37 us
    dot_general x2, matrix products, outer_sums(): lax.dot_general(weighted, right, (((0,), (0,)), ((), ())), precision=lax....  13.9 us
    unnamed x18, local copies, waits for them, and re-layouts  11 us

profile of v1, /device:TPU:0, one launch (start us, length us, event | category | flops | bytes accessed | tf_op | source)
XLA Modules:
  0.0 367.2 jit_solution(8424811427254098211)
XLA Ops:
  0.0 0.0 copy-start.1
  0.0 0.0 copy-start.2
  0.0 0.0 copy-start.3
  0.0 2.9 copy.36.po
  2.9 2.7 copy.37.pi
  5.6 0.0 copy-done.1
  5.6 1.2 copy.33.ph
  6.8 0.0 copy-done.2
  6.8 1.3 copy.34.pg
  8.1 0.0 copy-done.3
  8.1 1.2 copy.35.pu
  9.4 0.0 copy-start.5
  9.4 301.4 %gather_grads.1 = (f32[1024,64]{1,0:T(8,128)}, f32[1024,64]{1,0:T(8,128)}, f32[1024,64]{1,0:T(8,128)}, f32[1024,64]{1,0:T(8,128)}, f32[1024,64]{1,0:T(8,128)}) custom-call(bf16[256,8192]{1,0:T(8,128)(2,1)} %bitcast.40, bf16[3584,8192]{1,0:T(8,128)(2,1)} %w.1, bf16[1024,3584]{1,0:T(8,128)(2,1)} %bitcast.38, bf16[1024,3584]{1,0:T(8,128)(2,1)} %bitcast.39, ...), custom_call_target="tpu_custom_call" | custom-call | tf_op jit(solution)/shard_map/gather_grads/pallas_call | solution.py:244
  310.8 0.0 copy-start
  310.8 0.0 copy-start.4
  310.8 1.3 copy.40
  312.1 0.0 copy-done.5
  312.1 0.1 select_reduce_fusion
  312.2 0.1 fusion.20
  312.3 7.7 %fusion.10 = bf16[16,64,128]{1,2,0:T(8,128)(2,1)S(1)} fusion(f32[1024,64]{0,1:T(8,128)S(1)} %copy.40, f32[1024,16]{0,1:T(8,128)S(1)} %fusion.20, f32[1024,64]{1,0:T(8,128)} %get-tuple-element.14, f32[1024,64]{1,0:T(8,128)} %get-tuple-element.13), kind=kOutput, calls=%fused_computation.10 | convolution fusion | flops 1611923456 | bytes 1114112 | tf_op jit(solution)/shard_map/dot_general | solution.py:395
  320.0 0.0 copy-done
  320.0 0.2 copy.38
  320.2 0.0 copy-done.4
  320.2 6.2 %fusion.13 = bf16[16,64,64]{1,2,0:T(8,128)(2,1)S(1)} fusion(f32[1024,64]{0,1:T(8,128)S(1)} %copy.38, f32[1024,16]{0,1:T(8,128)S(1)} %fusion.20, f32[1024,64]{1,0:T(8,128)S(1)} %copy-done.4), kind=kOutput, calls=%fused_computation.11 | convolution fusion | flops 806420480 | bytes 720896 | tf_op jit(solution)/shard_map/dot_general | solution.py:395
  326.5 0.3 pad_maximum_fusion
  326.8 0.4 copy.42
  327.1 0.5 convert_element_type.13
  327.6 0.9 copy.48
  328.5 37.0 %exchange_scores.1 = f32[32,2048]{1,0:T(8,128)} custom-call(bf16[4,16,3072]{2,1,0:T(8,128)(2,1)} %bitcast.42, bf16[2048,3072]{1,0:T(8,128)(2,1)} %store_rows.1), custom_call_target="tpu_custom_call" | custom-call | tf_op jit(solution)/shard_map/exchange_scores/pallas_call | solution.py:370
  365.5 1.7 copy.50
  (2 shorter events, 0.0 us)
Async XLA Ops:
  0.0 5.6 %copy-start.1 = (bf16[3584,64]{0,1:T(8,128)(2,1)S(1)}, bf16[3584,64]{0,1:T(8,128)(2,1)}, u32[]{:S(2)}) copy-start(bf16[3584,64]{0,1:T(8,128)(2,1)} %param.18) | copy-start | bytes 1376260
  0.0 6.8 %copy-start.2 = (bf16[3584,64]{0,1:T(8,128)(2,1)S(1)}, bf16[3584,64]{0,1:T(8,128)(2,1)}, u32[]{:S(2)}) copy-start(bf16[3584,64]{0,1:T(8,128)(2,1)} %param.19) | copy-start | bytes 1376260
  0.0 8.1 %copy-start.3 = (bf16[3584,64]{0,1:T(8,128)(2,1)S(1)}, bf16[3584,64]{0,1:T(8,128)(2,1)}, u32[]{:S(2)}) copy-start(bf16[3584,64]{0,1:T(8,128)(2,1)} %param.20) | copy-start | bytes 1376260
  9.4 302.7 %copy-start.5 = (s32[1,16]{1,0:T(1,128)S(1)}, s32[1,16]{1,0:T(1,128)}, u32[]{:S(2)}) copy-start(s32[1,16]{1,0:T(1,128)} %param.16) | copy-start | bytes 196
  310.8 9.3 %copy-start = (f32[1024,64]{1,0:T(8,128)S(1)}, f32[1024,64]{1,0:T(8,128)}, u32[]{:S(2)}) copy-start(f32[1024,64]{1,0:T(8,128)} %get-tuple-element.10) | copy-start | bytes 786436
  310.8 9.5 %copy-start.4 = (f32[1024,64]{1,0:T(8,128)S(1)}, f32[1024,64]{1,0:T(8,128)}, u32[]{:S(2)}) copy-start(f32[1024,64]{1,0:T(8,128)} %get-tuple-element.11) | copy-start | bytes 786436

commit v2 on v1

--- a/solution.py
+++ b/solution.py
@@ -10,6 +10,7 @@
 MESH = pl.DeviceIdType.MESH
 NT = (((1,), (1,)), ((), ()))
 VMEM_LIMIT = 56 * 2**20
+CHUNKS = 4
 
 
 def tile_of(size, most):
@@ -18,9 +19,9 @@
 
 def gather_kernel(
     n, chunks, tile,
-    og, w, gate, up, ph, pg, pu, po, ni, pi,
-    down_in, gate_out, up_out, down_out, gate_in,
-    held, acc, gin, send_sem, recv_sem, local_sem, gin_send, gin_recv,
+    og, w, gate, up, ph, pg, pu, po, ni, pi, member,
+    down_sums, both_sums,
+    down_in, gate_out, up_out, down_out, held, acc, gin, send_sem, recv_sem, local_sem, gin_send, gin_recv,
 ):
     d = lax.axis_index("mp")
     tokens, width = og.shape
@@ -70,11 +71,13 @@
 
     lax.fori_loop(0, chunks, send_own, 0)
 
-    for ref in (down_in, gate_out, up_out, down_out):
+    for ref in (down_in, gate_out, up_out, down_out, down_sums, both_sums):
         ref[...] = jnp.zeros_like(ref)
 
     def own_gate_in(ni_ref, pi_ref):
-        part = jnp.dot(ni_ref[...], pi_ref[...], preferred_element_type=jnp.float32)
+        part = lax.dot_general(
+            ni_ref[...], pi_ref[...], NT, preferred_element_type=jnp.float32
+        )
         first = pl.program_id(0) == 0
 
         @pl.when(first)
@@ -90,7 +93,7 @@
         grid=(chunks,),
         in_specs=[
             pl.BlockSpec((tokens, depth), lambda c: (0, c)),
-            pl.BlockSpec((depth, pi.shape[1]), lambda c: (c, 0)),
+            pl.BlockSpec((pi.shape[0], depth), lambda c: (0, c)),
         ],
     )(ni, pi)
 
@@ -132,9 +135,10 @@
             for way in range(2):
                 @pl.when(valid[way])
                 def _():
-                    down_out[rows(at[way]), :] += jnp.dot(
+                    down_out[rows(at[way]), :] += lax.dot_general(
                         held[at[way], c],
-                        po[columns(c), :],
+                        po[:, columns(c)],
+                        NT,
                         preferred_element_type=jnp.float32,
                     )
 
@@ -192,12 +196,12 @@
                         (gate_out, gate_grad, pg_ref),
                         (up_out, up_grad, pu_ref),
                     ):
-                        out[at_rows, :] += jnp.dot(
-                            value, proj[...], preferred_element_type=jnp.float32
+                        out[at_rows, :] += lax.dot_general(
+                            value, proj[...], NT, preferred_element_type=jnp.float32
                         )
 
         elem = lambda way: pl.BlockSpec((tokens, tile), lambda j: (at[way], j))
-        proj = pl.BlockSpec((tile, ph.shape[1]), lambda j: (j, 0))
+        proj = pl.BlockSpec((ph.shape[0], tile), lambda j: (0, j))
         pltpu.emit_pipeline(
             finish,
             grid=(tiles,),
@@ -206,14 +210,38 @@
                 elem(0), elem(0), elem(1), elem(1), proj, proj, proj,
             ],
         )(w, gate, up, gate, up, ph, pg, pu)
+
+        @pl.when(s == 0)
+        def _():
+            for k in range(1, n):
+                gin_copy(k).wait()
+
+        for way in range(2):
+            @pl.when(valid[way])
+            def _():
+                at_rows = rows(at[way])
+                of = member[at[way]]
+
+                def add(sums, value, other):
+                    flat = value.T
+                    weighted = jnp.concatenate(
+                        [flat * of[e:e + 1, :] for e in range(of.shape[0])], axis=0
+                    )
+                    sums[...] += jnp.dot(
+                        weighted, other,
+                        precision=lax.Precision.HIGHEST,
+                        preferred_element_type=jnp.float32,
+                    )
+
+                add(down_sums, down_in[at_rows, :], down_out[at_rows, :])
+                add(
+                    both_sums, gin[at[way]],
+                    jnp.concatenate([gate_out[at_rows, :], up_out[at_rows, :]], axis=1),
+                )
+
         return carry
 
     lax.fori_loop(0, n, step, 0)
-
-    for k in range(1, n):
-        gin_copy(k).wait()
-    for p in range(n):
-        gate_in[p * tokens:(p + 1) * tokens, :] = gin[p]
 
     def drain(p, carry):
         def one(c, inner):
@@ -232,21 +260,25 @@
     lax.fori_loop(0, n, drain, 0)
 
 
-def gathered(n, og, w, gate, up, ph, pg, pu, po, ni, pi):
+def gathered(n, og, w, gate, up, ph, pg, pu, po, ni, pi, member):
     tokens, width = og.shape
-    units, r = ph.shape
-    chunks = 4
+    r, units = ph.shape
+    examples = member.shape[1]
+    chunks = CHUNKS
     depth = width // chunks
     tile = tile_of(units, 512)
-    out = jax.ShapeDtypeStruct((n * tokens, r), jnp.float32)
     hbm = pl.BlockSpec(memory_space=pl.ANY)
     vmem = pl.BlockSpec(memory_space=pltpu.VMEM)
     return pl.pallas_call(
         functools.partial(gather_kernel, n, chunks, tile),
-        out_shape=[out] * 5,
-        in_specs=[hbm] * 7 + [vmem, hbm, hbm],
-        out_specs=[vmem] * 5,
+        out_shape=[
+            jax.ShapeDtypeStruct((examples * r, r), jnp.float32),
+            jax.ShapeDtypeStruct((examples * r, 2 * r), jnp.float32),
+        ],
+        in_specs=[hbm] * 7 + [vmem, hbm, hbm, vmem],
+        out_specs=[vmem] * 2,
         scratch_shapes=[
+            *[pltpu.VMEM((n * tokens, r), jnp.float32)] * 4,
             pltpu.VMEM((n, chunks, tokens, depth), jnp.bfloat16),
             pltpu.VMEM((2, units // tile, tokens, tile), jnp.float32),
             pltpu.VMEM((n, tokens, r), jnp.float32),
@@ -260,7 +292,7 @@
             collective_id=0, has_side_effects=True, vmem_limit_bytes=VMEM_LIMIT
         ),
         name="gather_grads",
-    )(og, w, gate, up, ph, pg, pu, po, ni, pi)
+    )(og, w, gate, up, ph, pg, pu, po, ni, pi, member)
 
 
 def score_kernel(
@@ -302,10 +334,10 @@
 
     for k in range(1, n):
         feats_copy(k).start()
-    total = parts[d].astype(jnp.float32)
+    total = parts[d]
     for k in range(1, n):
         feats_copy(k).wait_recv()
-        total += feats_in[k - 1].astype(jnp.float32)
+        total += feats_in[k - 1]
     my_rows = pl.ds(pl.multiple_of(me * examples, examples), examples)
     queries[my_rows, :] = total.astype(jnp.bfloat16)
 
@@ -373,7 +405,7 @@
         in_specs=[vmem, pl.BlockSpec(memory_space=pl.ANY)],
         out_specs=vmem,
         scratch_shapes=[
-            pltpu.VMEM((n - 1, examples, width), jnp.bfloat16),
+            pltpu.VMEM((n - 1, examples, width), jnp.float32),
             pltpu.VMEM((replicas * examples, width), jnp.bfloat16),
             pltpu.VMEM(datastore.shape, jnp.bfloat16),
             pltpu.VMEM((n, block, count), sent),
@@ -388,18 +420,6 @@
         ),
         name="exchange_scores",
     )(parts, datastore)
-
-
-def outer_sums(member, left, right):
-    weighted = (member[:, :, None] * left[:, None, :]).reshape(left.shape[0], -1)
-    summed = lax.dot_general(
-        weighted,
-        right,
-        (((0,), (0,)), ((), ())),
-        precision=lax.Precision.HIGHEST,
-        preferred_element_type=jnp.float32,
-    )
-    return summed.reshape(member.shape[1], left.shape[1], right.shape[1])
 
 
 def on_device(
@@ -418,21 +438,18 @@
     starts = ends - example_lengths
     positions = jnp.arange(count, dtype=jnp.int32)
     member = (
-        (positions[:, None] >= starts[None, :]) & (positions[:, None] < ends[None, :])
+        (positions[None, :] >= starts[:, None]) & (positions[None, :] < ends[:, None])
     ).astype(jnp.float32)
 
-    down_in, gate_out, up_out, down_out, gate_in = gathered(
+    down, both = gathered(
         n, out_grad[0], w_down, gate_pre[0], up_pre[0],
-        proj_hidden, proj_gate, proj_up, proj_outgrad, normed_in[0], proj_input,
+        proj_hidden.T, proj_gate.T, proj_up.T, proj_outgrad.T, normed_in[0],
+        proj_input.T, member.reshape(examples, n, -1).transpose(1, 0, 2),
     )
-    down = outer_sums(member, down_in, down_out)
-    both = outer_sums(member, gate_in, jnp.concatenate([gate_out, up_out], axis=1))
+    down = down.reshape(examples, r, r)
+    both = both.reshape(examples, r, 2 * r)
     feats = jnp.concatenate([down, both[:, :, :r], both[:, :, r:]], axis=1)
-    parts = (
-        feats.astype(jnp.bfloat16)
-        .reshape(examples, n, -1)
-        .transpose(1, 0, 2)
-    )
+    parts = feats.reshape(examples, n, -1).transpose(1, 0, 2)
     return scored(n, stores, groups, parts, datastore)
 
 

time: 369 us -> 361 us (0.978)
  matrix products: 13.9 us -> 0 us
  Pallas kernels: 338 us -> 349 us
  local copies, waits for them, and re-layouts: 14.3 us -> 5.02 us
    dot_general x2 -> x0, matrix products: 13.9 us -> none  [outer_sums(): lax.dot_general(weighted, right, (((0,), (0,)), ((), ())), precision=lax....]
    unnamed x18 -> x1, local copies, waits for them, and re-layouts: 11 us -> 1.67 us
    pallas_call x1, Pallas kernels: 301 us -> 307 us  [gathered(): pl.pallas_call(functools.partial(gather_kernel, n, chunks, tile), out_sha...]
    pallas_call x1, Pallas kernels: 37 us -> 42 us  [scored(): pl.pallas_call(functools.partial(score_kernel, n, stores, groups, tile_of...]
where the time goes in v2:
time: 361 us; the launch traced here: 357 us
  Pallas kernels  349 us (97%)
  local copies, waits for them, and re-layouts  5.02 us (1%)
    pallas_call x1, Pallas kernels, gathered(): pl.pallas_call(functools.partial(gather_kernel, n, chunks, tile), out_sha...  307 us
    pallas_call x1, Pallas kernels, scored(): pl.pallas_call(functools.partial(score_kernel, n, stores, groups, tile_of...  42 us

profile of v2, /device:TPU:0, one launch (start us, length us, event | category | flops | bytes accessed | tf_op | source)
XLA Modules:
  0.0 357.1 jit_solution(3561703107331141940)
XLA Ops:
  0.0 0.8 select_reduce_fusion
  0.8 0.7 bitcast_subtract_fusion
  1.4 0.7 and_convert_fusion.member
  2.1 306.7 %gather_grads.1 = (f32[1024,64]{1,0:T(8,128)}, f32[1024,128]{1,0:T(8,128)}) custom-call(bf16[256,8192]{1,0:T(8,128)(2,1)} %bitcast.18, bf16[3584,8192]{1,0:T(8,128)(2,1)} %w.1, bf16[1024,3584]{1,0:T(8,128)(2,1)} %bitcast.16, bf16[1024,3584]{1,0:T(8,128)(2,1)} %bitcast.17, bf16[64,3584]{1,0:T(8,128)(2,1)} %bitcast.25, bf16[64,3584]{1,0:T(8,128)(2,1)} %bitcast.26, ...), custom_call_target="tpu_custom_call" | custom-call | tf_op jit(solution)/shard_map/gather_grads/pallas_call | solution.py:272
  308.9 1.4 fusion
  310.3 1.2 pad_maximum_fusion
  311.5 0.6 reshape.42
  312.1 1.3 copy.16
  313.4 42.0 %exchange_scores.1 = f32[32,2048]{1,0:T(8,128)} custom-call(f32[4,16,3072]{2,1,0:T(8,128)} %bitcast.20, bf16[2048,3072]{1,0:T(8,128)(2,1)} %store_rows.1), custom_call_target="tpu_custom_call" | custom-call | tf_op jit(solution)/shard_map/exchange_scores/pallas_call | solution.py:402
  355.4 1.7 copy.18
  (1 shorter events, 0.0 us)
